TPU v7x, 128 devices: a whole 4x4x4 slice. The times are simulated.
128 devices in a mesh: seq: 16 (over x, y), head: 8 (over z, core).
Axes of the slice: x: 4, y: 4, z: 4, core: 2. Of those that a mesh axis runs over, the one named last changes fastest.
Arguments:
- query: bfloat16 [4096, 4096], P('seq', 'head'), may hold values from -6 to 6
- key: bfloat16 [4096, 4096], P('seq', 'head'), may hold values from -6 to 6
- value: bfloat16 [4096, 4096], P('seq', 'head'), may hold values from -6 to 6
- head_gain: float32 [4096], P('head'), may hold values from 0.1 to 1.9
- out_weight: bfloat16 [4096, 4096], P('head', 'seq'), may hold values from -0.09375 to 0.09375
- stream: bfloat16 [4096, 4096], P(('seq', 'head')), may hold values from -6 to 6
- model_gain: float32 [4096], replicated, may hold values from 0.1 to 1.9
- expert_ids: int32 [4096, 8], P(('seq', 'head')), may hold values from 0 to 127, all different within a row; in each aligned block of 32 rows (0 to 31, 32 to 63, ...) at most 3 rows name the same one
- expert_gates: float32 [4096, 8], P(('seq', 'head')), may hold values from 0.1 to 0.5
- gate_weight: bfloat16 [128, 4096, 768], P(('seq', 'head')), may hold values from -0.09375 to 0.09375
- up_weight: bfloat16 [128, 4096, 768], P(('seq', 'head')), may hold values from -0.09375 to 0.09375
- down_weight: bfloat16 [128, 768, 4096], P(('seq', 'head')), may hold values from -0.21875 to 0.21875
- weight_scales: float32 [128, 3], P(('seq', 'head')), may hold values from 0.6 to 1.6
Outputs:
- layer_out: bfloat16 [4096, 4096], P(('seq', 'head'))
Inputs may be any that keep to these rules, and one draw needn't show every extreme that they name: `expert_ids`: among the 32 tokens of one device (aligned blocks of rows), no expert is named more than 3 times, a bound that some block reaches; the entries of one row differ.
All inputs are finite; a program needn't handle non-finite values.
Results may differ from a plain program's by a relative error of at most 0.013.
Values may be sent and summed in bfloat16 or wider, within the bound.
No kernel may reach another device: no remote copies, remote signals or barrier semaphores. Data moves between devices by JAX's collectives and lax.ppermute only.
A program may use at most 128 MiB of HBM per device.

v0:
```python
import jax
import jax.numpy as jnp
from jax import lax
from jax.sharding import PartitionSpec as P

D = 4096
HD = 128
TOPK = 8


def prefix(part, axis, combine, identity):
    place = lax.axis_index(axis)
    gathered = lax.all_gather(part, axis)
    state = jnp.zeros_like(part) + jnp.asarray(identity, part.dtype)

    def one(lap, state):
        return combine(state, lax.dynamic_index_in_dim(gathered, lap, 0, False))

    return lax.fori_loop(0, place, one, state)


def add_states(earlier, later):
    return earlier + later


def body(
    query,
    key,
    value,
    head_gain,
    out_weight,
    stream,
    model_gain,
    expert_ids,
    expert_gates,
    gate_weight,
    up_weight,
    down_weight,
    weight_scales,
):
    seq_rows = query.shape[0]
    heads_local = head_gain.shape[0] // HD
    query_rows = query.reshape(seq_rows, heads_local, HD)
    key_rows = key.reshape(seq_rows, heads_local, HD)
    value_rows = value.reshape(seq_rows, heads_local, HD)
    scores = jnp.einsum("thd,shd->hts", query_rows, key_rows, preferred_element_type=jnp.float32)
    causal = jnp.tril(jnp.ones((seq_rows, seq_rows), dtype=bool))
    scores = jnp.where(causal[None, :, :], scores, 0.0).astype(jnp.bfloat16)
    local_part = jnp.einsum("hts,shd->thd", scores, value_rows, preferred_element_type=jnp.float32)
    block_state = jnp.einsum(
        "shd,she->hde", key_rows, value_rows, preferred_element_type=jnp.float32
    )
    prior_state = prefix(block_state, "seq", add_states, jnp.zeros_like(block_state))
    earlier_part = jnp.einsum(
        "thd,hde->the",
        query_rows,
        prior_state.astype(jnp.bfloat16),
        preferred_element_type=jnp.float32,
    )
    mixed_heads = local_part + earlier_part
    mean_square = jnp.mean(mixed_heads * mixed_heads, axis=-1, keepdims=True)
    head_normed = (
        mixed_heads * lax.rsqrt(mean_square + 1e-06) * head_gain.reshape(heads_local, HD)
    ).astype(jnp.bfloat16)
    head_normed = head_normed.reshape(seq_rows, heads_local * HD)
    full_out = lax.all_gather(out_weight, "seq", axis=1, tiled=True)
    tok_rows = stream.shape[0]
    attention = lax.psum_scatter(
        jnp.dot(head_normed, full_out, preferred_element_type=jnp.float32),
        "head",
        scatter_dimension=0,
        tiled=True,
    )
    residual_float = (
        (stream.astype(jnp.float32) + attention).astype(jnp.bfloat16).astype(jnp.float32)
    )
    mean_square = jnp.mean(residual_float * residual_float, axis=-1, keepdims=True)
    normed = (residual_float * lax.rsqrt(mean_square + 1e-06) * model_gain).astype(jnp.bfloat16)
    seq_count = lax.axis_size("seq")
    head_count = lax.axis_size("head")
    experts = seq_count * head_count
    capacity = 3 * tok_rows * TOPK // (2 * experts)
    flat_ids = expert_ids.reshape(-1)
    onehot = (flat_ids[:, None] == jnp.arange(experts, dtype=jnp.int32)[None, :]).astype(jnp.int32)
    earlier_count = jnp.cumsum(onehot, axis=0) - onehot
    slot_index = jnp.sum(earlier_count * onehot, axis=1)
    target = flat_ids * capacity + slot_index
    source_rows = jnp.broadcast_to(normed[:, None, :], (tok_rows, TOPK, D)).reshape(
        tok_rows * TOPK, D
    )
    outgoing = jnp.zeros((experts * capacity, D), jnp.bfloat16).at[target].set(source_rows)
    outgoing = outgoing.reshape(experts, capacity, D)
    scale_row = weight_scales[0]
    slot_rows = lax.all_to_all(outgoing, ("seq", "head"), split_axis=0, concat_axis=0, tiled=True)
    gate_part = (
        jnp.einsum("smd,df->smf", slot_rows, gate_weight[0], preferred_element_type=jnp.float32)
        * scale_row[0]
    )
    up_part = (
        jnp.einsum("smd,df->smf", slot_rows, up_weight[0], preferred_element_type=jnp.float32)
        * scale_row[1]
    )
    act = (jax.nn.silu(gate_part) * up_part).astype(jnp.bfloat16)
    produced = (
        jnp.einsum("smf,fd->smd", act, down_weight[0], preferred_element_type=jnp.float32)
        * scale_row[2]
    )
    computed = produced.astype(jnp.bfloat16)
    results = lax.all_to_all(computed, ("seq", "head"), split_axis=0, concat_axis=0, tiled=True)
    gathered = results.reshape(experts * capacity, D)[target].reshape(tok_rows, TOPK, D)
    expert_mix = jnp.sum(gathered.astype(jnp.float32) * expert_gates[:, :, None], axis=1)
    return (residual_float + expert_mix).astype(jnp.bfloat16)


def solution(mesh):
    return jax.shard_map(
        body,
        mesh=mesh,
        in_specs=(
            P("seq", "head"),
            P("seq", "head"),
            P("seq", "head"),
            P("head"),
            P("head", "seq"),
            P(("seq", "head"), None),
            P(),
            P(("seq", "head"), None),
            P(("seq", "head"), None),
            P(("seq", "head"), None, None),
            P(("seq", "head"), None, None),
            P(("seq", "head"), None, None),
            P(("seq", "head"), None),
        ),
        out_specs=P(("seq", "head"), None),
        check_vma=False,
    )
```

profile of v0, /device:TPU:1, one launch (start us, length us, event | category | flops | bytes accessed | tf_op | source)
XLA Modules:
  0.0 346.8 jit_solution(17948770530914740345)
XLA Ops:
  6.5 0.0 copy-start
  6.5 0.0 all-gather.6.cloned.1.call-start
  6.5 1.1 copy.50
  7.7 1.9 fusion.46
  9.5 0.0 copy-start.3
  9.5 0.0 all-gather.6.cloned.1.call-update
  9.6 0.0 all-gather.4.cloned.1.call-start
  9.6 0.7 all-gather.4.cloned.1.call-update
  10.3 0.0 reduce-scatter.2.cloned.1.call-start
  10.4 53.9 %all-gather.6.cloned.1.call-done = f32[64,128,128]{2,1,0:T(8,128)} async-done(((f32[4,128,128]{2,1,0:T(8,128)}), f32[64,128,128]{2,1,0:T(8,128)}) %all-gather.6.cloned.1.call-update) | async-done | bytes 4194320 | tf_op jit(solution)/shard_map/all_gather | solution.py:13
  64.3 0.0 copy-start.9
  64.4 0.0 copy-done
  64.4 0.3 convolution_bitcast_fusion
  64.7 0.0 copy-done.3
  64.7 0.5 multiply_reduce_fusion
  65.2 0.0 copy-done.9
  65.2 0.1 multiply_convert_fusion.1
  65.3 57.4 %all-gather.4.cloned.1.call-done = bf16[512,4096]{1,0:T(8,128)(2,1)} async-done(((bf16[512,256]{1,0:T(8,128)(2,1)}), bf16[512,4096]{1,0:T(8,128)(2,1)}) %all-gather.4.cloned.1.call-update) | async-done | bytes 4194320 | tf_op jit(solution)/shard_map/all_gather | solution.py:66
  122.7 5.4 %fusion.66 = f32[256,4096]{1,0:T(8,128)} fusion(bf16[256,512]{0,1:T(8,128)(2,1)S(1)} %bitcast.95, bf16[512,4096]{1,0:T(8,128)(2,1)} %all-gather.4.cloned.1.call-done), kind=kOutput, calls=%fused_computation.68 | convolution fusion | flops 1073741824 | bytes 8650752 | tf_op jit(solution)/shard_map/dot_general | solution.py:69
  128.2 0.0 copy-start.6
  128.2 0.0 copy-start.4
  128.2 0.0 copy-start.5
  128.2 0.0 reduce-scatter.2.cloned.1.call-update
  128.2 0.7 copy-done.6
  128.9 0.1 copy.41
  128.9 0.1 eq.29
  129.0 0.1 eq.25
  129.1 0.1 copy.43
  129.2 0.2 fusion.56
  129.5 0.1 copy.40
  129.6 0.1 mul.100
  129.7 0.2 fusion.58
  129.9 34.0 %reduce-scatter.2.cloned.1.call-done = f32[32,4096]{1,0:T(8,128)} async-done(((f32[256,4096]{1,0:T(8,128)}), f32[32,4096]{1,0:T(8,128)}) %reduce-scatter.2.cloned.1.call-update) | async-done | bytes 524304 | tf_op jit(solution)/shard_map/reduce_scatter | solution.py:68
  163.9 0.0 copy-done.4
  163.9 1.2 fusion.39
  165.1 0.0 copy-start.2
  165.1 0.0 copy-done.5
  165.1 0.8 fusion.41
  166.0 4.8 %scatter_custom_fusion = bf16[384,4096]{1,0:T(8,128)(2,1)S(1)} fusion(s32[256]{0:T(256)S(1)} %bitcast.103, bf16[]{:T(256)} %constant.40.clone.1, bf16[32,4096]{1,0:T(8,128)(2,1)} %fusion.41), kind=kCustom, calls=%fused_computation.14 | custom fusion | bytes 3407874 | tf_op jit(solution)/shard_map/scatter | solution.py:91
  170.8 4.5 %reshape.109 = bf16[128,3,4096]{2,1,0:T(4,128)(2,1)} reshape(bf16[384,4096]{1,0:T(8,128)(2,1)S(1)} %scatter_custom_fusion) | data formatting | bytes 6291456 | tf_op jit(solution)/shard_map/reshape | solution.py:92
  175.3 0.0 copy-done.2
  175.3 10.5 %all-to-all-start = ((bf16[128,3,4096]{2,1,0:T(4,128)(2,1)}), bf16[128,3,4096]{2,1,0:T(4,128)(2,1)}, u32[]{:S(2)}, u32[]{:S(2)}) async-start(bf16[128,3,4096]{2,1,0:T(4,128)(2,1)} %reshape.109), calls=%async_computation.1 | async-start | bytes 8388608 | tf_op jit(solution)/shard_map/all_to_all | solution.py:94
  185.8 0.0 copy-done.7
  185.8 0.6 fusion.63
  186.4 52.1 %all-to-all-done = bf16[128,3,4096]{2,1,0:T(4,128)(2,1)} async-done(((bf16[128,3,4096]{2,1,0:T(4,128)(2,1)}), bf16[128,3,4096]{2,1,0:T(4,128)(2,1)}, u32[]{:S(2)}, u32[]{:S(2)}) %all-to-all-start) | async-done | bytes 3145760 | tf_op jit(solution)/shard_map/all_to_all | solution.py:94
  238.6 11.5 %fusion.14 = f32[128,3,768]{2,0,1:T(8,128)S(1)} fusion(bf16[1,4096,768]{2,1,0:T(8,128)(2,1)} %param.24, bf16[128,3,4096]{2,1,0:T(4,128)(2,1)} %all-to-all-done, f32[]{:T(128)} %bitcast.14), kind=kOutput, calls=%fused_computation.17 | convolution fusion | flops 2416214016 | bytes 10616836 | tf_op jit(solution)/shard_map/smd,df->smf/dot_general | solution.py:96
  250.1 0.0 slice-done
  250.1 0.0 slice-done.1
  250.2 0.0 slice-start.3
  250.2 8.8 %fusion.29 = bf16[128,3,768]{2,0,1:T(8,128)(2,1)S(1)} fusion(bf16[1,4096,768]{2,1,0:T(8,128)(2,1)S(1)} %bitcast.107, bf16[128,3,4096]{2,1,0:T(4,128)(2,1)} %all-to-all-done, f32[128,3,768]{2,0,1:T(8,128)S(1)} %fusion.14, f32[]{:T(128)} %bitcast.17), kind=kOutput, calls=%fused_computation.21 | convolution fusion | flops 2417983488 | bytes 11206660 | tf_op jit(solution)/shard_map/smd,df->smf/dot_general | solution.py:100
  258.9 0.0 slice-done.2
  259.0 0.0 slice-done.3
  259.0 3.7 %multiply_convert_fusion = bf16[128,3,4096]{2,0,1:T(8,128)(2,1)S(1)} fusion(bf16[128,3,768]{2,0,1:T(8,128)(2,1)S(1)} %fusion.29, bf16[1,768,4096]{2,1,0:T(8,128)(2,1)S(1)} %bitcast.109, f32[]{:T(128)} %bitcast.20), kind=kOutput, calls=%fused_computation.9 | convolution fusion | flops 2419064832 | bytes 10027012 | tf_op jit(solution)/shard_map/smf,fd->smd/dot_general | solution.py:105
  262.7 4.7 %copy.47 = bf16[128,3,4096]{2,1,0:T(4,128)(2,1)} copy(bf16[128,3,4096]{2,0,1:T(8,128)(2,1)S(1)} %multiply_convert_fusion) | data formatting | bytes 6291456 | tf_op jit(solution)/shard_map/convert_element_type | solution.py:108
  267.4 5.8 %all-to-all-start.1 = ((bf16[128,3,4096]{2,1,0:T(4,128)(2,1)}), bf16[128,3,4096]{2,1,0:T(4,128)(2,1)}, u32[]{:S(2)}, u32[]{:S(2)}) async-start(bf16[128,3,4096]{2,1,0:T(4,128)(2,1)} %copy.47), calls=%async_computation.2 | async-start | bytes 8388608 | tf_op jit(solution)/shard_map/all_to_all | solution.py:109
  273.2 0.0 copy-done.8
  273.2 0.1 copy.48
  273.3 52.8 %all-to-all-done.1 = bf16[128,3,4096]{2,1,0:T(4,128)(2,1)} async-done(((bf16[128,3,4096]{2,1,0:T(4,128)(2,1)}), bf16[128,3,4096]{2,1,0:T(4,128)(2,1)}, u32[]{:S(2)}, u32[]{:S(2)}) %all-to-all-start.1) | async-done | bytes 3145760 | tf_op jit(solution)/shard_map/all_to_all | solution.py:109
  326.1 6.0 %reshape.110 = bf16[384,4096]{1,0:T(8,128)(2,1)S(1)} reshape(bf16[128,3,4096]{2,1,0:T(4,128)(2,1)} %all-to-all-done.1) | data formatting | bytes 6291456 | tf_op jit(solution)/shard_map/reshape | solution.py:110
  332.1 0.0 copy-start.1
  332.1 3.2 gather_fusion
  335.3 3.2 fusion.8
  338.5 1.7 fusion.42
  340.2 0.0 copy-done.1
  (21 shorter events, 0.2 us)
Async XLA Ops:
  6.5 57.8 %copy-start = (bf16[256,512]{1,0:T(8,128)(2,1)S(1)}, bf16[256,512]{1,0:T(8,128)(2,1)}, u32[]{:S(2)}) copy-start(bf16[256,512]{1,0:T(8,128)(2,1)} %param.15) | copy-start | bytes 786436
  6.5 57.8 %all-gather.6.cloned.1.call-start = ((), (), s32[]{:S(2)}) async-start(), calls=%async_computation.5 | async-start | bytes 4456448 | tf_op jit(solution)/shard_map/all_gather | solution.py:13
  9.5 55.1 %copy-start.3 = (bf16[256,512]{1,0:T(8,128)(2,1)S(1)}, bf16[256,512]{1,0:T(8,128)(2,1)}, u32[]{:S(2)}) copy-start(bf16[256,512]{1,0:T(8,128)(2,1)} %param.17) | copy-start | bytes 786436
  9.6 113.2 %all-gather.4.cloned.1.call-start = ((), (), s32[]{:S(2)}) async-start(), calls=%async_computation.3 | async-start | bytes 4456448 | tf_op jit(solution)/shard_map/all_gather | solution.py:66
  10.3 153.6 %reduce-scatter.2.cloned.1.call-start = ((), (), s32[]{:S(2)}) async-start(), calls=%async_computation.4 | async-start | bytes 4718592 | tf_op jit(solution)/shard_map/reduce_scatter | solution.py:68
  64.3 0.8 copy-start.9
  128.2 0.7 copy-start.6
  128.2 35.7 %copy-start.4 = (bf16[32,4096]{1,0:T(8,128)(2,1)S(1)}, bf16[32,4096]{1,0:T(8,128)(2,1)}, u32[]{:S(2)}) copy-start(bf16[32,4096]{1,0:T(8,128)(2,1)} %param.20) | copy-start | bytes 786436
  128.2 37.0 %copy-start.5 = (f32[4096]{0:T(1024)S(1)}, f32[4096]{0:T(1024)}, u32[]{:S(2)}) copy-start(f32[4096]{0:T(1024)} %param.21) | copy-start | bytes 49156
  165.1 10.2 %copy-start.2 = (bf16[32,4096]{1,0:T(8,128)(2,1)}, bf16[32,4096]{1,0:T(8,128)(2,1)S(1)}, u32[]{:S(2)}) copy-start(bf16[32,4096]{1,0:T(8,128)(2,1)S(1)} %get-tuple-element.38) | copy-start | bytes 786436
  175.3 10.5 %copy-start.7 = (f32[1,3]{1,0:T(1,128)S(1)}, f32[1,3]{1,0:T(1,128)}, u32[]{:S(2)}) copy-start(f32[1,3]{1,0:T(1,128)} %param.27) | copy-start | bytes 40
  175.3 74.8 %slice-start = ((s8[6291456]{0:T(1024)(128)(4,1)}), s8[2097152]{0:T(1024)(128)(4,1)S(1)}, s32[]{:S(2)}) async-start(s8[6291456]{0:T(1024)(128)(4,1)} %bitcast.106), calls=%async_computation.6 | async-start | bytes 4194304
  175.3 63.2 %all-to-all-start = ((bf16[128,3,4096]{2,1,0:T(4,128)(2,1)}), bf16[128,3,4096]{2,1,0:T(4,128)(2,1)}, u32[]{:S(2)}, u32[]{:S(2)}) async-start(bf16[128,3,4096]{2,1,0:T(4,128)(2,1)} %reshape.109), calls=%async_computation.1 | async-start | bytes 8388608 | tf_op jit(solution)/shard_map/all_to_all | solution.py:94
  238.6 11.6 %slice-start.1 = ((s8[6291456]{0:T(1024)(128)(4,1)}), s8[4194304]{0:T(1024)(128)(4,1)S(1)}, s32[]{:S(2)}) async-start(s8[6291456]{0:T(1024)(128)(4,1)} %bitcast.106), calls=%async_computation.7 | async-start | bytes 8388608
  238.6 20.4 %slice-start.2 = ((s8[6291456]{0:T(1024)(128)(4,1)}), s8[4194304]{0:T(1024)(128)(4,1)S(1)}, s32[]{:S(2)}) async-start(s8[6291456]{0:T(1024)(128)(4,1)} %bitcast.108), calls=%async_computation.8 | async-start | bytes 8388608
  250.2 8.8 %slice-start.3 = ((s8[6291456]{0:T(1024)(128)(4,1)}), s8[2097152]{0:T(1024)(128)(4,1)S(1)}, s32[]{:S(2)}) async-start(s8[6291456]{0:T(1024)(128)(4,1)} %bitcast.108), calls=%async_computation.9 | async-start | bytes 4194304
  267.4 5.8 %copy-start.8 = (f32[32,8]{0,1:T(8,128)S(1)}, f32[32,8]{0,1:T(8,128)}, u32[]{:S(2)}) copy-start(f32[32,8]{0,1:T(8,128)} %param.23) | copy-start | bytes 3076
  267.4 58.7 %all-to-all-start.1 = ((bf16[128,3,4096]{2,1,0:T(4,128)(2,1)}), bf16[128,3,4096]{2,1,0:T(4,128)(2,1)}, u32[]{:S(2)}, u32[]{:S(2)}) async-start(bf16[128,3,4096]{2,1,0:T(4,128)(2,1)} %copy.47), calls=%async_computation.2 | async-start | bytes 8388608 | tf_op jit(solution)/shard_map/all_to_all | solution.py:109
  332.1 8.1 %copy-start.1 = (bf16[256,512]{1,0:T(8,128)(2,1)S(1)}, bf16[256,512]{1,0:T(8,128)(2,1)}, u32[]{:S(2)}) copy-start(bf16[256,512]{1,0:T(8,128)(2,1)} %param.15) | copy-start | bytes 786436
Sparse Core Ops, SparseCore 0:
  9.7 54.5 all-gather.5
  66.4 56.2 all-gather.3
  128.3 35.5 reduce-scatter.1
where the time goes:
time: 348 us; the launch traced here: 347 us
  waiting for transfers between devices  251 us (72%)
  matrix products  32.1 us (9%)
  local copies, waits for them, and re-layouts  26.2 us (8%)
  starting transfers between devices  16.4 us (5%)
  between operations  13.4 us (4%)
  other arithmetic  7.63 us (2%)
    all_gather x1, waiting for transfers between devices, body(): full_out = lax.all_gather(out_weight, 'seq', axis=1, tiled=True)  57.4 us
    all_gather x1, waiting for transfers between devices, prefix(): gathered = lax.all_gather(part, axis)  53.9 us
    all_to_all x1, waiting for transfers between devices, body(): lax.all_to_all(computed, ('seq', 'head'), split_axis=0, concat_axis=0, ti...  52.8 us
    all_to_all x1, waiting for transfers between devices, body(): lax.all_to_all(outgoing, ('seq', 'head'), split_axis=0, concat_axis=0, ti...  52.1 us
    reduce_scatter x1, waiting for transfers between devices, body(): lax.psum_scatter(jnp.dot(head_normed, full_out, preferred_element_type=jn...  34 us
    dot_general x1, matrix products, body(): jnp.einsum('smd,df->smf', slot_rows, gate_weight[0], preferred_element_ty...  11.5 us
    all_to_all x1, starting transfers between devices, body(): lax.all_to_all(outgoing, ('seq', 'head'), split_axis=0, concat_axis=0, ti...  10.5 us
    dot_general x1, matrix products, body(): jnp.einsum('smd,df->smf', slot_rows, up_weight[0], preferred_element_type...  8.77 us
  transfers between devices with their start and end apart: 5, of which 5 were waited for; matrix products, arithmetic and copies ran while one was open for 1% of the time, Pallas kernels for 0%

commit v1 on v0

--- a/solution.py
+++ b/solution.py
@@ -6,6 +6,28 @@
 D = 4096
 HD = 128
 TOPK = 8
+
+
+def laid_out(blocks, dim):
+    blocks = jnp.moveaxis(blocks, 0, dim)
+    dims = blocks.shape
+    return blocks.reshape(*dims[:dim], dims[dim] * dims[dim + 1], *dims[dim + 2 :])
+
+
+def doubled(x, axis):
+    size = lax.axis_size(axis)
+    pieces = x[None]
+    for level in range(size.bit_length() - 1):
+        bit = 1 << level
+        other = lax.ppermute(pieces, axis, [(i, i ^ bit) for i in range(size)])
+        both = jnp.stack([pieces, other])
+        upper = lax.axis_index(axis) >> level & 1
+        pieces = jnp.where(upper == 0, both, both[::-1]).reshape(-1, *x.shape)
+    return pieces
+
+
+def collect(value, axis, dim):
+    return laid_out(doubled(value, axis), dim)
 
 
 def prefix(part, axis, combine, identity):
@@ -63,7 +85,7 @@
         mixed_heads * lax.rsqrt(mean_square + 1e-06) * head_gain.reshape(heads_local, HD)
     ).astype(jnp.bfloat16)
     head_normed = head_normed.reshape(seq_rows, heads_local * HD)
-    full_out = lax.all_gather(out_weight, "seq", axis=1, tiled=True)
+    full_out = collect(out_weight, "seq", 1)
     tok_rows = stream.shape[0]
     attention = lax.psum_scatter(
         jnp.dot(head_normed, full_out, preferred_element_type=jnp.float32),

time: 348 us -> 374 us (1.075)
  starting transfers between devices: 16.4 us -> 24.9 us
  waiting for transfers between devices: 251 us -> 258 us
  other arithmetic: 7.63 us -> 14.6 us
    ppermute x0 -> x4, waiting for transfers between devices: none -> 99 us  [doubled(): other = lax.ppermute(pieces, axis, [(i, i ^ bit) for i in range(size)])]
    all_gather x1 -> x0, waiting for transfers between devices: 57.4 us -> none  [body(): full_out = lax.all_gather(out_weight, 'seq', axis=1, tiled=True)]
    all_gather x1, waiting for transfers between devices: 53.9 us -> 0.01 us  [prefix(): gathered = lax.all_gather(part, axis)]
    reduce_scatter x1, waiting for transfers between devices: 34 us -> 54.1 us  [body(): lax.psum_scatter(jnp.dot(head_normed, full_out, preferred_element_type=jn...]
    ppermute x0 -> x4, starting transfers between devices: none -> 8.57 us  [doubled(): other = lax.ppermute(pieces, axis, [(i, i ^ bit) for i in range(size)])]
  transfers between devices with their start and end apart: 5 -> 8, of which waited for: 5 -> 7; matrix products, arithmetic and copies ran while one was open for 1% -> 3% of each run, Pallas kernels for 0% -> 0%
where the time goes in v1:
time: 374 us; the launch traced here: 372 us
  waiting for transfers between devices  258 us (69%)
  matrix products  31.9 us (9%)
  local copies, waits for them, and re-layouts  29.2 us (8%)
  starting transfers between devices  24.9 us (7%)
  other arithmetic  14.6 us (4%)
  between operations  13.7 us (4%)
    ppermute x4, waiting for transfers between devices, doubled(): other = lax.ppermute(pieces, axis, [(i, i ^ bit) for i in range(size)])  99 us
    reduce_scatter x1, waiting for transfers between devices, body(): lax.psum_scatter(jnp.dot(head_normed, full_out, preferred_element_type=jn...  54.1 us
    all_to_all x1, waiting for transfers between devices, body(): lax.all_to_all(computed, ('seq', 'head'), split_axis=0, concat_axis=0, ti...  52.8 us
    all_to_all x1, waiting for transfers between devices, body(): lax.all_to_all(outgoing, ('seq', 'head'), split_axis=0, concat_axis=0, ti...  52.2 us
    dot_general x1, matrix products, body(): jnp.einsum('smd,df->smf', slot_rows, gate_weight[0], preferred_element_ty...  11.5 us
    all_to_all x1, starting transfers between devices, body(): lax.all_to_all(outgoing, ('seq', 'head'), split_axis=0, concat_axis=0, ti...  10.5 us
    dot_general x1, matrix products, body(): jnp.einsum('smd,df->smf', slot_rows, up_weight[0], preferred_element_type...  8.68 us
    ppermute x4, starting transfers between devices, doubled(): other = lax.ppermute(pieces, axis, [(i, i ^ bit) for i in range(size)])  8.57 us
  transfers between devices with their start and end apart: 8, of which 7 were waited for; matrix products, arithmetic and copies ran while one was open for 3% of the time, Pallas kernels for 0%

profile of v1, /device:TPU:1, one launch (start us, length us, event | category | flops | bytes accessed | tf_op | source)
XLA Modules:
  0.0 372.5 jit_solution(18246483683381244955)
XLA Ops:
  6.5 0.0 copy-start
  6.5 0.0 all-gather.3.cloned.1.call-start
  6.5 1.1 copy.54
  7.7 1.9 fusion.48
  9.5 0.0 all-gather.3.cloned.1.call-update
  9.6 0.0 reduce-scatter.2.cloned.1.call-start
  9.6 2.2 collective-permute-start
  11.8 5.8 %collective-permute-done = bf16[1,512,256]{2,1,0:T(8,128)(2,1)S(1)} collective-permute-done((bf16[1,512,256]{2,1,0:T(8,128)(2,1)}, bf16[1,512,256]{2,1,0:T(8,128)(2,1)S(1)}, u32[]{:S(2)}, u32[]{:S(2)}) %collective-permute-start) | collective-permute-done | bytes 262176 | tf_op jit(solution)/shard_map/ppermute | solution.py:22
  17.6 1.0 pad_maximum_fusion.3
  18.6 0.1 fusion.46
  18.8 3.3 collective-permute-start.1
  22.0 14.5 %collective-permute-done.1 = bf16[2,512,256]{2,1,0:T(8,128)(2,1)S(1)} collective-permute-done((bf16[2,512,256]{2,1,0:T(8,128)(2,1)S(1)}, bf16[2,512,256]{2,1,0:T(8,128)(2,1)S(1)}, u32[]{:S(2)}, u32[]{:S(2)}) %collective-permute-start.1) | collective-permute-done | bytes 524320 | tf_op jit(solution)/shard_map/ppermute | solution.py:22
  36.5 0.1 pad_maximum_fusion.2
  36.6 0.2 reverse_select_fusion.2
  36.8 1.1 collective-permute-start.2
  37.9 28.7 %collective-permute-done.2 = bf16[4,512,256]{2,1,0:T(8,128)(2,1)S(1)} collective-permute-done((bf16[4,512,256]{2,1,0:T(8,128)(2,1)S(1)}, bf16[4,512,256]{2,1,0:T(8,128)(2,1)S(1)}, u32[]{:S(2)}, u32[]{:S(2)}) %collective-permute-start.2) | collective-permute-done | bytes 1048608 | tf_op jit(solution)/shard_map/ppermute | solution.py:22
  66.6 0.2 pad_maximum_fusion.1
  66.8 0.4 reverse_select_fusion.1
  67.2 2.4 copy.42
  69.6 2.0 collective-permute-start.3
  71.7 50.0 %collective-permute-done.3 = bf16[8,512,256]{1,2,0:T(8,128)(2,1)S(1)} collective-permute-done((bf16[8,512,256]{1,2,0:T(8,128)(2,1)}, bf16[8,512,256]{1,2,0:T(8,128)(2,1)S(1)}, u32[]{:S(2)}, u32[]{:S(2)}) %collective-permute-start.3) | collective-permute-done | bytes 2097184 | tf_op jit(solution)/shard_map/ppermute | solution.py:22
  121.7 2.0 pad_maximum_fusion
  123.7 2.9 reverse_select_fusion
  126.6 0.0 copy-start.9
  126.7 0.0 copy-done
  126.7 0.3 convolution_bitcast_fusion
  127.0 0.6 copy-done.3
  127.6 0.5 multiply_reduce_fusion
  128.1 0.0 copy-done.9
  128.1 0.1 multiply_convert_fusion.1
  128.2 5.4 %fusion.68 = f32[256,4096]{1,0:T(8,128)} fusion(bf16[256,512]{0,1:T(8,128)(2,1)S(1)} %bitcast.120, bf16[512,4096]{0,1:T(8,128)(2,1)} %bitcast.114), kind=kOutput, calls=%fused_computation.78 | convolution fusion | flops 1073741824 | bytes 8650752 | tf_op jit(solution)/shard_map/dot_general | solution.py:91
  133.7 0.0 reduce-scatter.2.cloned.1.call-update
  133.7 0.7 copy-done.6
  134.4 0.1 copy.45
  134.4 0.1 eq.45
  134.5 0.1 eq.41
  134.6 0.1 copy.44
  134.7 0.1 mul.100
  134.8 0.1 copy.47
  134.9 0.2 fusion.58
  135.2 0.2 fusion.60
  135.4 54.1 %reduce-scatter.2.cloned.1.call-done = f32[32,4096]{1,0:T(8,128)} async-done(((f32[256,4096]{1,0:T(8,128)}), f32[32,4096]{1,0:T(8,128)}) %reduce-scatter.2.cloned.1.call-update) | async-done | bytes 524304 | tf_op jit(solution)/shard_map/reduce_scatter | solution.py:90
  189.5 1.2 fusion.39
  190.7 0.8 fusion.41
  191.6 4.8 %scatter_custom_fusion = bf16[384,4096]{1,0:T(8,128)(2,1)S(1)} fusion(s32[256]{0:T(256)S(1)} %bitcast.133, bf16[]{:T(256)} %constant.46.clone.1, bf16[32,4096]{1,0:T(8,128)(2,1)} %fusion.41), kind=kCustom, calls=%fused_computation.18 | custom fusion | bytes 3407874 | tf_op jit(solution)/shard_map/scatter | solution.py:113
  196.4 4.5 %reshape.129 = bf16[128,3,4096]{2,1,0:T(4,128)(2,1)} reshape(bf16[384,4096]{1,0:T(8,128)(2,1)S(1)} %scatter_custom_fusion) | data formatting | bytes 6291456 | tf_op jit(solution)/shard_map/reshape | solution.py:114
  200.9 10.5 %all-to-all-start = ((bf16[128,3,4096]{2,1,0:T(4,128)(2,1)}), bf16[128,3,4096]{2,1,0:T(4,128)(2,1)}, u32[]{:S(2)}, u32[]{:S(2)}) async-start(bf16[128,3,4096]{2,1,0:T(4,128)(2,1)} %reshape.129), calls=%async_computation.1 | async-start | bytes 8388608 | tf_op jit(solution)/shard_map/all_to_all | solution.py:116
  211.3 0.0 copy-done.7
  211.4 0.6 fusion.65
  211.9 52.2 %all-to-all-done = bf16[128,3,4096]{2,1,0:T(4,128)(2,1)} async-done(((bf16[128,3,4096]{2,1,0:T(4,128)(2,1)}), bf16[128,3,4096]{2,1,0:T(4,128)(2,1)}, u32[]{:S(2)}, u32[]{:S(2)}) %all-to-all-start) | async-done | bytes 3145760 | tf_op jit(solution)/shard_map/all_to_all | solution.py:116
  264.1 11.5 %fusion.14 = f32[128,3,768]{2,0,1:T(8,128)S(1)} fusion(bf16[1,4096,768]{2,1,0:T(8,128)(2,1)} %param.24, bf16[128,3,4096]{2,1,0:T(4,128)(2,1)} %all-to-all-done, f32[]{:T(128)} %bitcast.29), kind=kOutput, calls=%fused_computation.22 | convolution fusion | flops 2416214016 | bytes 10616836 | tf_op jit(solution)/shard_map/smd,df->smf/dot_general | solution.py:118
  275.6 0.0 slice-start.3
  275.7 8.7 %fusion.29 = bf16[128,3,768]{2,0,1:T(8,128)(2,1)S(1)} fusion(bf16[1,4096,768]{2,1,0:T(8,128)(2,1)S(1)} %bitcast.137, bf16[128,3,4096]{2,1,0:T(4,128)(2,1)} %all-to-all-done, f32[128,3,768]{2,0,1:T(8,128)S(1)} %fusion.14, f32[]{:T(128)} %bitcast.32), kind=kOutput, calls=%fused_computation.26 | convolution fusion | flops 2417983488 | bytes 11206660 | tf_op jit(solution)/shard_map/smd,df->smf/dot_general | solution.py:122
  284.4 3.7 multiply_convert_fusion
  288.1 4.7 %copy.51 = bf16[128,3,4096]{2,1,0:T(4,128)(2,1)} copy(bf16[128,3,4096]{2,0,1:T(8,128)(2,1)S(1)} %multiply_convert_fusion) | data formatting | bytes 6291456 | tf_op jit(solution)/shard_map/convert_element_type | solution.py:130
  292.8 5.8 %all-to-all-start.1 = ((bf16[128,3,4096]{2,1,0:T(4,128)(2,1)}), bf16[128,3,4096]{2,1,0:T(4,128)(2,1)}, u32[]{:S(2)}, u32[]{:S(2)}) async-start(bf16[128,3,4096]{2,1,0:T(4,128)(2,1)} %copy.51), calls=%async_computation.2 | async-start | bytes 8388608 | tf_op jit(solution)/shard_map/all_to_all | solution.py:131
  298.6 0.1 copy.52
  298.7 52.8 %all-to-all-done.1 = bf16[128,3,4096]{2,1,0:T(4,128)(2,1)} async-done(((bf16[128,3,4096]{2,1,0:T(4,128)(2,1)}), bf16[128,3,4096]{2,1,0:T(4,128)(2,1)}, u32[]{:S(2)}, u32[]{:S(2)}) %all-to-all-start.1) | async-done | bytes 3145760 | tf_op jit(solution)/shard_map/all_to_all | solution.py:131
  351.5 6.0 %reshape.130 = bf16[384,4096]{1,0:T(8,128)(2,1)S(1)} reshape(bf16[128,3,4096]{2,1,0:T(4,128)(2,1)} %all-to-all-done.1) | data formatting | bytes 6291456 | tf_op jit(solution)/shard_map/reshape | solution.py:132
  357.5 0.0 copy-start.1
  357.5 3.2 gather_fusion
  360.7 3.2 fusion.8
  363.9 1.7 fusion.42
  365.6 0.0 copy-done.1
  (35 shorter events, 0.2 us)
Async XLA Ops:
  6.5 120.1 %copy-start = (bf16[256,512]{1,0:T(8,128)(2,1)S(1)}, bf16[256,512]{1,0:T(8,128)(2,1)}, u32[]{:S(2)}) copy-start(bf16[256,512]{1,0:T(8,128)(2,1)} %param.15) | copy-start | bytes 786436
  6.5 120.1 %all-gather.3.cloned.1.call-start = ((), (), s32[]{:S(2)}) async-start(), calls=%async_computation.4 | async-start | bytes 4456448 | tf_op jit(solution)/shard_map/all_gather | solution.py:35
  9.6 179.9 %reduce-scatter.2.cloned.1.call-start = ((), (), s32[]{:S(2)}) async-start(), calls=%async_computation.3 | async-start | bytes 4718592 | tf_op jit(solution)/shard_map/reduce_scatter | solution.py:90
  9.6 8.0 %collective-permute-start = (bf16[1,512,256]{2,1,0:T(8,128)(2,1)}, bf16[1,512,256]{2,1,0:T(8,128)(2,1)S(1)}, u32[]{:S(2)}, u32[]{:S(2)}) collective-permute-start(bf16[1,512,256]{2,1,0:T(8,128)(2,1)} %bitcast.128), channel_id=1, source_target_pairs={{0,8},{8,0},{16,24},{24,16},{32,40},{40,32},{48,56},{56,48},{64,72... | collective-permute-start | bytes 786440 | tf_op jit(solution)/shard_map/ppermute | solution.py:22
  18.8 17.7 %collective-permute-start.1 = (bf16[2,512,256]{2,1,0:T(8,128)(2,1)S(1)}, bf16[2,512,256]{2,1,0:T(8,128)(2,1)S(1)}, u32[]{:S(2)}, u32[]{:S(2)}) collective-permute-start(bf16[2,512,256]{2,1,0:T(8,128)(2,1)S(1)} %get-tuple-element.40), channel_id=1, source_target_pairs={{0,16},{8,24},{16,0},{24,8},{32,48},{40,56},{48,32},{56,40},{64,80... | collective-permute-start | bytes 1572872 | tf_op jit(solution)/shard_map/ppermute | solution.py:22
  36.8 29.8 %collective-permute-start.2 = (bf16[4,512,256]{2,1,0:T(8,128)(2,1)S(1)}, bf16[4,512,256]{2,1,0:T(8,128)(2,1)S(1)}, u32[]{:S(2)}, u32[]{:S(2)}) collective-permute-start(bf16[4,512,256]{2,1,0:T(8,128)(2,1)S(1)} %bitcast.117), channel_id=1, source_target_pairs={{0,32},{8,40},{16,48},{24,56},{32,0},{40,8},{48,16},{56,24},{64,96... | collective-permute-start | bytes 3145736 | tf_op jit(solution)/shard_map/ppermute | solution.py:22
  69.6 52.1 %collective-permute-start.3 = (bf16[8,512,256]{1,2,0:T(8,128)(2,1)}, bf16[8,512,256]{1,2,0:T(8,128)(2,1)S(1)}, u32[]{:S(2)}, u32[]{:S(2)}) collective-permute-start(bf16[8,512,256]{1,2,0:T(8,128)(2,1)} %bitcast.115), channel_id=1, source_target_pairs={{0,64},{8,72},{16,80},{24,88},{32,96},{40,104},{48,112},{56,120},{... | collective-permute-start | bytes 6291464 | tf_op jit(solution)/shard_map/ppermute | solution.py:22
  126.6 0.9 copy-start.3
  126.6 1.4 copy-start.9
  133.7 0.7 copy-start.6
  133.7 55.8 %copy-start.4 = (bf16[32,4096]{1,0:T(8,128)(2,1)S(1)}, bf16[32,4096]{1,0:T(8,128)(2,1)}, u32[]{:S(2)}) copy-start(bf16[32,4096]{1,0:T(8,128)(2,1)} %param.20) | copy-start | bytes 786436
  133.7 57.0 %copy-start.5 = (f32[4096]{0:T(1024)S(1)}, f32[4096]{0:T(1024)}, u32[]{:S(2)}) copy-start(f32[4096]{0:T(1024)} %param.21) | copy-start | bytes 49156
  190.7 10.2 %copy-start.2 = (bf16[32,4096]{1,0:T(8,128)(2,1)}, bf16[32,4096]{1,0:T(8,128)(2,1)S(1)}, u32[]{:S(2)}) copy-start(bf16[32,4096]{1,0:T(8,128)(2,1)S(1)} %get-tuple-element.38) | copy-start | bytes 786436
  200.9 10.5 %copy-start.7 = (f32[1,3]{1,0:T(1,128)S(1)}, f32[1,3]{1,0:T(1,128)}, u32[]{:S(2)}) copy-start(f32[1,3]{1,0:T(1,128)} %param.27) | copy-start | bytes 40
  200.9 74.8 %slice-start = ((s8[6291456]{0:T(1024)(128)(4,1)}), s8[2097152]{0:T(1024)(128)(4,1)S(1)}, s32[]{:S(2)}) async-start(s8[6291456]{0:T(1024)(128)(4,1)} %bitcast.136), calls=%async_computation.5 | async-start | bytes 4194304
  200.9 63.3 %all-to-all-start = ((bf16[128,3,4096]{2,1,0:T(4,128)(2,1)}), bf16[128,3,4096]{2,1,0:T(4,128)(2,1)}, u32[]{:S(2)}, u32[]{:S(2)}) async-start(bf16[128,3,4096]{2,1,0:T(4,128)(2,1)} %reshape.129), calls=%async_computation.1 | async-start | bytes 8388608 | tf_op jit(solution)/shard_map/all_to_all | solution.py:116
  264.1 11.5 %slice-start.1 = ((s8[6291456]{0:T(1024)(128)(4,1)}), s8[4194304]{0:T(1024)(128)(4,1)S(1)}, s32[]{:S(2)}) async-start(s8[6291456]{0:T(1024)(128)(4,1)} %bitcast.136), calls=%async_computation.6 | async-start | bytes 8388608
  264.1 20.2 %slice-start.2 = ((s8[6291456]{0:T(1024)(128)(4,1)}), s8[4194304]{0:T(1024)(128)(4,1)S(1)}, s32[]{:S(2)}) async-start(s8[6291456]{0:T(1024)(128)(4,1)} %bitcast.138), calls=%async_computation.7 | async-start | bytes 8388608
  275.6 8.7 %slice-start.3 = ((s8[6291456]{0:T(1024)(128)(4,1)}), s8[2097152]{0:T(1024)(128)(4,1)S(1)}, s32[]{:S(2)}) async-start(s8[6291456]{0:T(1024)(128)(4,1)} %bitcast.138), calls=%async_computation.8 | async-start | bytes 4194304
  292.8 5.8 %copy-start.8 = (f32[32,8]{0,1:T(8,128)S(1)}, f32[32,8]{0,1:T(8,128)}, u32[]{:S(2)}) copy-start(f32[32,8]{0,1:T(8,128)} %param.23) | copy-start | bytes 3076
  292.8 58.7 %all-to-all-start.1 = ((bf16[128,3,4096]{2,1,0:T(4,128)(2,1)}), bf16[128,3,4096]{2,1,0:T(4,128)(2,1)}, u32[]{:S(2)}, u32[]{:S(2)}) async-start(bf16[128,3,4096]{2,1,0:T(4,128)(2,1)} %copy.51), calls=%async_computation.2 | async-start | bytes 8388608 | tf_op jit(solution)/shard_map/all_to_all | solution.py:131
  357.5 8.2 %copy-start.1 = (bf16[256,512]{1,0:T(8,128)(2,1)S(1)}, bf16[256,512]{1,0:T(8,128)(2,1)}, u32[]{:S(2)}) copy-start(bf16[256,512]{1,0:T(8,128)(2,1)} %param.15) | copy-start | bytes 786436
Sparse Core Ops, SparseCore 0:
  9.7 71.8 all-gather.2
  133.8 55.6 reduce-scatter.1
